TPU v7x, 256 devices: a whole 4x4x8 slice. The times are simulated.
256 devices in a mesh: guide: 64 (over z, x, y_hi), face: 4 (over y_lo, core).
Axes of the slice: x: 4, y: 4 (y_hi: 2, y_lo: 2; y = y_hi * 2 + y_lo), z: 8, core: 2. Of those that a mesh axis runs over, the one named last changes fastest.
Arguments:
- transfer: bfloat16 [64, 1024, 1024], P('guide'), may hold values from -0.2 to 1.2
- leaf_map: bfloat16 [64, 1024, 4096], P('guide'), may hold values from -0.09375 to 0.09375
- volume_source: bfloat16 [64, 1024, 4096], P('guide', 'face'), may hold values from -6 to 6
Outputs:
- traces: bfloat16 [64, 1024, 1024], P('guide', 'face')
All inputs are finite; a program needn't handle non-finite values.
Results may differ from a plain program's by a relative error of at most 0.02.
Values may be sent and summed in bfloat16 or wider, within the bound.
No kernel may reach another device: no remote copies, remote signals or barrier semaphores. Data moves between devices by JAX's collectives and lax.ppermute only.
A program may use at most 128 MiB of HBM per device.

v0:
```python
import jax
import jax.numpy as jnp
from jax import lax
from jax.sharding import PartitionSpec as P


def passed_along(block, axis, distance):
    devices = range(lax.axis_size(axis))
    route = [((i - distance) % len(devices), i) for i in devices]
    return lax.ppermute(block, axis, route)


def from_partner(block, axis, distance):
    count = lax.axis_size(axis)
    route = []
    for low in range(count):
        high = low | 1 << distance
        if high != low and high < count:
            route += [(low, high), (high, low)]
    return lax.ppermute(block, axis, route)


def apply_map(linear_map, vectors):
    return lax.dot_general(
        vectors, linear_map, (((1,), (1,)), ((), ())), preferred_element_type=jnp.float32
    )


def pass_on(moving):
    return passed_along(moving, "guide", 4)


def merge_level(own_map, own_trace, level_bit, is_upper):
    face_count = lax.axis_size("face")
    row_count = own_map.shape[0] // face_count
    row_start = lax.axis_index("face") * row_count
    other_map, other_trace = from_partner((own_map, own_trace), "guide", level_bit)
    upper_map = jnp.where(is_upper, own_map, other_map)
    lower_map = jnp.where(is_upper, other_map, own_map)
    upper_trace = jnp.where(is_upper, own_trace, other_trace)
    lower_trace = jnp.where(is_upper, other_trace, own_trace)
    upper_rows = lax.dynamic_slice_in_dim(upper_map, row_start, row_count, 0)
    row_block = jnp.dot(upper_rows, lower_map, preferred_element_type=jnp.float32).astype(
        jnp.bfloat16
    )
    merged_map = lax.all_gather(row_block, "face", axis=0, tiled=True)
    merged_trace = (apply_map(upper_map, lower_trace) + upper_trace.astype(jnp.float32)).astype(
        jnp.bfloat16
    )
    return (merged_map, merged_trace, lower_map, lower_trace)


def local(transfer, leaf_map, volume_source):
    own_map = transfer[0]
    source = lax.dot_general(
        volume_source[0], leaf_map[0], (((1,), (1,)), ((), ())), preferred_element_type=jnp.float32
    ).astype(jnp.bfloat16)
    position = lax.axis_index("guide")
    pair_upper = position % 2 == 1
    group_upper = position // 2 % 2 == 1
    first_map, first_trace, pair_map, pair_trace = merge_level(own_map, source, 0, pair_upper)
    group_map, group_trace, half_map, half_trace = merge_level(
        first_map, first_trace, 1, group_upper
    )
    turns = lax.axis_size("guide") // 4 - 1

    def advance(turn_index, moving):
        arrived = pass_on(moving)
        return (apply_map(group_map, arrived) + group_trace.astype(jnp.float32)).astype(
            jnp.bfloat16
        )

    entering = pass_on(lax.fori_loop(0, turns, advance, group_trace))
    second = (apply_map(half_map, entering) + half_trace.astype(jnp.float32)).astype(jnp.bfloat16)
    lifted = jnp.where(group_upper, second, entering)
    outer = (apply_map(pair_map, lifted) + pair_trace.astype(jnp.float32)).astype(jnp.bfloat16)
    traces = jnp.where(pair_upper, outer, lifted)
    return traces[None]


def solution(mesh):
    in_specs = (P("guide", None, None), P("guide", None, None), P("guide", "face", None))
    out_specs = P("guide", "face", None)
    return jax.shard_map(local, mesh=mesh, in_specs=in_specs, out_specs=out_specs, check_vma=False)
```

profile of v0, /device:TPU:18, one launch (start us, length us, event | category | flops | bytes accessed | tf_op | source)
XLA Modules:
  0.0 484.9 jit_solution(10789300844934941388)
XLA Ops:
  6.5 0.3 collective-permute-start.2
  6.9 48.9 %collective-permute-done.2 = bf16[1024,1024]{1,0:T(8,128)(2,1)} collective-permute-done((bf16[1024,1024]{1,0:T(8,128)(2,1)}, bf16[1024,1024]{1,0:T(8,128)(2,1)}, u32[]{:S(2)}, u32[]{:S(2)}) %collective-permute-start.2) | collective-permute-done | bytes 2097184 | tf_op jit(solution)/shard_map/ppermute | solution.py:20
  55.7 1.8 broadcast_select_fusion.3
  57.6 1.3 copy-done.4
  58.9 3.1 convolution_convert_fusion.1
  62.1 34.1 %all-gather.3.cloned.1.call-done = bf16[1024,1024]{1,0:T(8,128)(2,1)} async-done(((bf16[256,1024]{1,0:T(8,128)(2,1)}), bf16[1024,1024]{1,0:T(8,128)(2,1)}) %all-gather.3.cloned.1.call-update) | async-done | bytes 2097168 | tf_op jit(solution)/shard_map/all_gather | solution.py:46
  96.1 0.6 collective-permute-start.4
  96.7 47.7 %collective-permute-done.4 = bf16[1024,1024]{1,0:T(8,128)(2,1)} collective-permute-done((bf16[1024,1024]{1,0:T(8,128)(2,1)}, bf16[1024,1024]{1,0:T(8,128)(2,1)}, u32[]{:S(2)}, u32[]{:S(2)}) %collective-permute-start.4) | collective-permute-done | bytes 2097184 | tf_op jit(solution)/shard_map/ppermute | solution.py:20
  144.4 1.8 broadcast_select_fusion.1
  146.3 1.4 copy-done.6
  147.7 3.1 convolution_convert_fusion
  150.8 5.9 %fusion.4 = bf16[256,1024]{1,0:T(8,128)(2,1)S(1)} fusion(bf16[1,1024,4096]{2,1,0:T(8,128)(2,1)} %param.6, bf16[1,256,4096]{2,1,0:T(8,128)(2,1)S(1)} %copy-done), kind=kOutput, calls=%fused_computation.13 | convolution fusion | flops 2147745792 | bytes 11010048 | tf_op jit(solution)/shard_map/dot_general | solution.py:55
  156.7 0.9 collective-permute-start.1
  157.6 21.3 %collective-permute-done.1 = bf16[256,1024]{1,0:T(8,128)(2,1)S(1)} collective-permute-done((bf16[256,1024]{1,0:T(8,128)(2,1)S(1)}, bf16[256,1024]{1,0:T(8,128)(2,1)S(1)}, u32[]{:S(2)}, u32[]{:S(2)}) %collective-permute-start.1) | collective-permute-done | bytes 524320 | tf_op jit(solution)/shard_map/ppermute | solution.py:20
  178.9 0.8 fusion.9
  179.8 9.9 %collective-permute-done.3 = bf16[256,1024]{1,0:T(8,128)(2,1)S(1)} collective-permute-done((bf16[256,1024]{1,0:T(8,128)(2,1)S(1)}, bf16[256,1024]{1,0:T(8,128)(2,1)S(1)}, u32[]{:S(2)}, u32[]{:S(2)}) %collective-permute-start.3) | collective-permute-done | bytes 524320 | tf_op jit(solution)/shard_map/ppermute | solution.py:20
  189.7 0.8 fusion.10
  190.6 268.7 %while.10 = (s32[]{:T(128)}, bf16[256,1024]{1,0:T(8,128)(2,1)S(1)}, bf16[1024,1024]{1,0:T(8,128)(2,1)}, bf16[256,1024]{1,0:T(8,128)(2,1)S(1)}, s32[]{:T(128)}) while((s32[]{:T(128)}, bf16[256,1024]{1,0:T(8,128)(2,1)S(1)}, bf16[1024,1024]{1,0:T(8,128)(2,1)}, bf16[256,1024]{1,0:T(8,128)(2,1)S(1)}, s32[]{:T(128)}) %tuple.18), condition=%wide.region_1.2_spmd, body=%wide.region_0.1_spmd.sunk | while | flops 537657344 | bytes 5767269 | solution.py:73
  190.6 2.2 collective-permute-start
  192.7 15.8 %collective-permute-done = bf16[256,1024]{1,0:T(8,128)(2,1)} collective-permute-done((bf16[256,1024]{1,0:T(8,128)(2,1)S(1)}, bf16[256,1024]{1,0:T(8,128)(2,1)}, u32[]{:S(2)}, u32[]{:S(2)}) %collective-permute-start) | collective-permute-done | bytes 524320 | tf_op jit(solution)/shard_map/while/body/eval_jaxpr/ppermute | solution.py:10
  208.5 2.5 fusion.33
  211.1 0.1 collective-permute-start
  211.1 15.7 %collective-permute-done = bf16[256,1024]{1,0:T(8,128)(2,1)} collective-permute-done((bf16[256,1024]{1,0:T(8,128)(2,1)S(1)}, bf16[256,1024]{1,0:T(8,128)(2,1)}, u32[]{:S(2)}, u32[]{:S(2)}) %collective-permute-start) | collective-permute-done | bytes 524320 | tf_op jit(solution)/shard_map/while/body/eval_jaxpr/ppermute | solution.py:10
  226.9 2.5 fusion.33
  229.4 4.5 collective-permute-start
  233.9 11.7 %collective-permute-done = bf16[256,1024]{1,0:T(8,128)(2,1)} collective-permute-done((bf16[256,1024]{1,0:T(8,128)(2,1)S(1)}, bf16[256,1024]{1,0:T(8,128)(2,1)}, u32[]{:S(2)}, u32[]{:S(2)}) %collective-permute-start) | collective-permute-done | bytes 524320 | tf_op jit(solution)/shard_map/while/body/eval_jaxpr/ppermute | solution.py:10
  245.6 2.5 fusion.33
  248.1 3.1 collective-permute-start
  251.2 14.2 %collective-permute-done = bf16[256,1024]{1,0:T(8,128)(2,1)} collective-permute-done((bf16[256,1024]{1,0:T(8,128)(2,1)S(1)}, bf16[256,1024]{1,0:T(8,128)(2,1)}, u32[]{:S(2)}, u32[]{:S(2)}) %collective-permute-start) | collective-permute-done | bytes 524320 | tf_op jit(solution)/shard_map/while/body/eval_jaxpr/ppermute | solution.py:10
  265.5 2.5 fusion.33
  268.0 0.8 collective-permute-start
  268.8 17.6 %collective-permute-done = bf16[256,1024]{1,0:T(8,128)(2,1)} collective-permute-done((bf16[256,1024]{1,0:T(8,128)(2,1)S(1)}, bf16[256,1024]{1,0:T(8,128)(2,1)}, u32[]{:S(2)}, u32[]{:S(2)}) %collective-permute-start) | collective-permute-done | bytes 524320 | tf_op jit(solution)/shard_map/while/body/eval_jaxpr/ppermute | solution.py:10
  286.4 2.5 fusion.33
  289.0 0.1 collective-permute-start
  289.1 17.6 %collective-permute-done = bf16[256,1024]{1,0:T(8,128)(2,1)} collective-permute-done((bf16[256,1024]{1,0:T(8,128)(2,1)S(1)}, bf16[256,1024]{1,0:T(8,128)(2,1)}, u32[]{:S(2)}, u32[]{:S(2)}) %collective-permute-start) | collective-permute-done | bytes 524320 | tf_op jit(solution)/shard_map/while/body/eval_jaxpr/ppermute | solution.py:10
  306.7 2.5 fusion.33
  309.2 0.1 collective-permute-start
  309.3 16.8 %collective-permute-done = bf16[256,1024]{1,0:T(8,128)(2,1)} collective-permute-done((bf16[256,1024]{1,0:T(8,128)(2,1)S(1)}, bf16[256,1024]{1,0:T(8,128)(2,1)}, u32[]{:S(2)}, u32[]{:S(2)}) %collective-permute-start) | collective-permute-done | bytes 524320 | tf_op jit(solution)/shard_map/while/body/eval_jaxpr/ppermute | solution.py:10
  326.1 2.5 fusion.33
  328.7 0.1 collective-permute-start
  328.8 15.9 %collective-permute-done = bf16[256,1024]{1,0:T(8,128)(2,1)} collective-permute-done((bf16[256,1024]{1,0:T(8,128)(2,1)S(1)}, bf16[256,1024]{1,0:T(8,128)(2,1)}, u32[]{:S(2)}, u32[]{:S(2)}) %collective-permute-start) | collective-permute-done | bytes 524320 | tf_op jit(solution)/shard_map/while/body/eval_jaxpr/ppermute | solution.py:10
  344.7 2.5 fusion.33
  347.3 15.0 %collective-permute-done = bf16[256,1024]{1,0:T(8,128)(2,1)} collective-permute-done((bf16[256,1024]{1,0:T(8,128)(2,1)S(1)}, bf16[256,1024]{1,0:T(8,128)(2,1)}, u32[]{:S(2)}, u32[]{:S(2)}) %collective-permute-start) | collective-permute-done | bytes 524320 | tf_op jit(solution)/shard_map/while/body/eval_jaxpr/ppermute | solution.py:10
  362.3 2.5 fusion.33
  364.9 14.0 %collective-permute-done = bf16[256,1024]{1,0:T(8,128)(2,1)} collective-permute-done((bf16[256,1024]{1,0:T(8,128)(2,1)S(1)}, bf16[256,1024]{1,0:T(8,128)(2,1)}, u32[]{:S(2)}, u32[]{:S(2)}) %collective-permute-start) | collective-permute-done | bytes 524320 | tf_op jit(solution)/shard_map/while/body/eval_jaxpr/ppermute | solution.py:10
  378.9 2.5 fusion.33
  381.4 0.1 collective-permute-start
  381.5 13.1 %collective-permute-done = bf16[256,1024]{1,0:T(8,128)(2,1)} collective-permute-done((bf16[256,1024]{1,0:T(8,128)(2,1)S(1)}, bf16[256,1024]{1,0:T(8,128)(2,1)}, u32[]{:S(2)}, u32[]{:S(2)}) %collective-permute-start) | collective-permute-done | bytes 524320 | tf_op jit(solution)/shard_map/while/body/eval_jaxpr/ppermute | solution.py:10
  394.7 2.5 fusion.33
  397.2 0.1 collective-permute-start
  397.3 12.9 %collective-permute-done = bf16[256,1024]{1,0:T(8,128)(2,1)} collective-permute-done((bf16[256,1024]{1,0:T(8,128)(2,1)S(1)}, bf16[256,1024]{1,0:T(8,128)(2,1)}, u32[]{:S(2)}, u32[]{:S(2)}) %collective-permute-start) | collective-permute-done | bytes 524320 | tf_op jit(solution)/shard_map/while/body/eval_jaxpr/ppermute | solution.py:10
  410.2 2.5 fusion.33
  412.7 0.1 collective-permute-start
  412.8 12.9 %collective-permute-done = bf16[256,1024]{1,0:T(8,128)(2,1)} collective-permute-done((bf16[256,1024]{1,0:T(8,128)(2,1)S(1)}, bf16[256,1024]{1,0:T(8,128)(2,1)}, u32[]{:S(2)}, u32[]{:S(2)}) %collective-permute-start) | collective-permute-done | bytes 524320 | tf_op jit(solution)/shard_map/while/body/eval_jaxpr/ppermute | solution.py:10
  425.7 2.5 fusion.33
  428.2 0.1 collective-permute-start
  428.3 12.9 %collective-permute-done = bf16[256,1024]{1,0:T(8,128)(2,1)} collective-permute-done((bf16[256,1024]{1,0:T(8,128)(2,1)S(1)}, bf16[256,1024]{1,0:T(8,128)(2,1)}, u32[]{:S(2)}, u32[]{:S(2)}) %collective-permute-start) | collective-permute-done | bytes 524320 | tf_op jit(solution)/shard_map/while/body/eval_jaxpr/ppermute | solution.py:10
  441.2 2.5 fusion.33
  443.7 0.1 collective-permute-start
  443.8 12.9 %collective-permute-done = bf16[256,1024]{1,0:T(8,128)(2,1)} collective-permute-done((bf16[256,1024]{1,0:T(8,128)(2,1)S(1)}, bf16[256,1024]{1,0:T(8,128)(2,1)}, u32[]{:S(2)}, u32[]{:S(2)}) %collective-permute-start) | collective-permute-done | bytes 524320 | tf_op jit(solution)/shard_map/while/body/eval_jaxpr/ppermute | solution.py:10
  456.7 2.5 fusion.33
  459.4 12.8 %collective-permute-done.5 = bf16[256,1024]{1,0:T(8,128)(2,1)S(1)} collective-permute-done((bf16[256,1024]{1,0:T(8,128)(2,1)S(1)}, bf16[256,1024]{1,0:T(8,128)(2,1)S(1)}, u32[]{:S(2)}, u32[]{:S(2)}) %collective-permute-start.5) | collective-permute-done | bytes 524320 | tf_op jit(solution)/shard_map/ppermute | solution.py:10
  472.1 2.6 fusion.12
  474.7 3.3 fusion.15
  (36 shorter events, 0.5 us)
Async XLA Ops:
  6.5 144.3 %copy-start = (bf16[1,256,4096]{2,1,0:T(8,128)(2,1)S(1)}, bf16[1,256,4096]{2,1,0:T(8,128)(2,1)}, u32[]{:S(2)}) copy-start(bf16[1,256,4096]{2,1,0:T(8,128)(2,1)} %param.7) | copy-start | bytes 6291460
  6.5 89.6 %all-gather.3.cloned.1.call-start = ((), (), s32[]{:S(2)}) async-start(), calls=%async_computation | async-start | bytes 2621440 | tf_op jit(solution)/shard_map/all_gather | solution.py:46
  6.5 49.2 %collective-permute-start.2 = (bf16[1024,1024]{1,0:T(8,128)(2,1)}, bf16[1024,1024]{1,0:T(8,128)(2,1)}, u32[]{:S(2)}, u32[]{:S(2)}) collective-permute-start(bf16[1024,1024]{1,0:T(8,128)(2,1)} %bitcast.32), channel_id=1, source_target_pairs={{0,4},{4,0},{8,12},{12,8},{16,20},{20,16},{24,28},{28,24},{32,36},... | collective-permute-start | bytes 6291464 | tf_op jit(solution)/shard_map/ppermute | solution.py:20
  6.9 52.0 %copy-start.1 = (bf16[1,1024,1024]{2,1,0:T(8,128)(2,1)S(1)}, bf16[1,1024,1024]{2,1,0:T(8,128)(2,1)}, u32[]{:S(2)}) copy-start(bf16[1,1024,1024]{2,1,0:T(8,128)(2,1)} %param.5) | copy-start | bytes 6291460
  57.5 1.3 copy-start.4
  62.0 128.5 %all-gather.5.cloned.1.call-start = ((), (), s32[]{:S(2)}) async-start(), calls=%async_computation.1 | async-start | bytes 2621440 | tf_op jit(solution)/shard_map/all_gather | solution.py:46
  96.1 48.3 %collective-permute-start.4 = (bf16[1024,1024]{1,0:T(8,128)(2,1)}, bf16[1024,1024]{1,0:T(8,128)(2,1)}, u32[]{:S(2)}, u32[]{:S(2)}) collective-permute-start(bf16[1024,1024]{1,0:T(8,128)(2,1)} %all-gather.3.cloned.1.call-done), channel_id=1, source_target_pairs={{0,8},{8,0},{4,12},{12,4},{16,24},{24,16},{20,28},{28,20},{32,40},... | collective-permute-start | bytes 6291464 | tf_op jit(solution)/shard_map/ppermute | solution.py:20
  96.7 51.0 %copy-start.3 = (bf16[1024,1024]{1,0:T(8,128)(2,1)S(1)}, bf16[1024,1024]{1,0:T(8,128)(2,1)}, u32[]{:S(2)}) copy-start(bf16[1024,1024]{1,0:T(8,128)(2,1)} %all-gather.3.cloned.1.call-done) | copy-start | bytes 6291460
  146.3 1.4 copy-start.6
  150.8 28.1 %copy-start.5 = (bf16[1024,1024]{1,0:T(8,128)(2,1)S(1)}, bf16[1024,1024]{1,0:T(8,128)(2,1)}, u32[]{:S(2)}) copy-start(bf16[1024,1024]{1,0:T(8,128)(2,1)} %copy-done.4) | copy-start | bytes 6291460
  156.7 22.9 %copy-start.8 = (bf16[256,1024]{1,0:T(8,128)(2,1)}, bf16[256,1024]{1,0:T(8,128)(2,1)S(1)}, u32[]{:S(2)}) copy-start(bf16[256,1024]{1,0:T(8,128)(2,1)S(1)} %fusion.4) | copy-start | bytes 1572868
  156.7 33.0 %copy-start.7 = (bf16[1024,1024]{1,0:T(8,128)(2,1)S(1)}, bf16[1024,1024]{1,0:T(8,128)(2,1)}, u32[]{:S(2)}) copy-start(bf16[1024,1024]{1,0:T(8,128)(2,1)} %copy-done.6) | copy-start | bytes 6291460
  156.7 22.2 %collective-permute-start.1 = (bf16[256,1024]{1,0:T(8,128)(2,1)S(1)}, bf16[256,1024]{1,0:T(8,128)(2,1)S(1)}, u32[]{:S(2)}, u32[]{:S(2)}) collective-permute-start(bf16[256,1024]{1,0:T(8,128)(2,1)S(1)} %fusion.4), channel_id=1, source_target_pairs={{0,4},{4,0},{8,12},{12,8},{16,20},{20,16},{24,28},{28,24},{32,36},... | collective-permute-start | bytes 1572872 | tf_op jit(solution)/shard_map/ppermute | solution.py:20
  178.9 0.8 copy-start.10
  179.7 10.7 %copy-start.12 = (bf16[256,1024]{1,0:T(8,128)(2,1)}, bf16[256,1024]{1,0:T(8,128)(2,1)S(1)}, u32[]{:S(2)}) copy-start(bf16[256,1024]{1,0:T(8,128)(2,1)S(1)} %fusion.9) | copy-start | bytes 1572868
  179.7 10.0 %collective-permute-start.3 = (bf16[256,1024]{1,0:T(8,128)(2,1)S(1)}, bf16[256,1024]{1,0:T(8,128)(2,1)S(1)}, u32[]{:S(2)}, u32[]{:S(2)}) collective-permute-start(bf16[256,1024]{1,0:T(8,128)(2,1)S(1)} %fusion.9), channel_id=1, source_target_pairs={{0,8},{8,0},{4,12},{12,4},{16,24},{24,16},{20,28},{28,20},{32,40},... | collective-permute-start | bytes 1572872 | tf_op jit(solution)/shard_map/ppermute | solution.py:20
  189.7 0.8 copy-start.13
  190.6 18.0 %collective-permute-start = (bf16[256,1024]{1,0:T(8,128)(2,1)S(1)}, bf16[256,1024]{1,0:T(8,128)(2,1)}, u32[]{:S(2)}, u32[]{:S(2)}) collective-permute-start(bf16[256,1024]{1,0:T(8,128)(2,1)S(1)} %get-tuple-element.67), channel_id=1, source_target_pairs={{240,0},{244,4},{248,8},{252,12},{0,16},{4,20},{8,24},{12,28},{16,... | collective-permute-start | bytes 1572872 | tf_op jit(solution)/shard_map/while/body/eval_jaxpr/ppermute | solution.py:10
  211.1 15.8 %collective-permute-start = (bf16[256,1024]{1,0:T(8,128)(2,1)S(1)}, bf16[256,1024]{1,0:T(8,128)(2,1)}, u32[]{:S(2)}, u32[]{:S(2)}) collective-permute-start(bf16[256,1024]{1,0:T(8,128)(2,1)S(1)} %get-tuple-element.67), channel_id=1, source_target_pairs={{240,0},{244,4},{248,8},{252,12},{0,16},{4,20},{8,24},{12,28},{16,... | collective-permute-start | bytes 1572872 | tf_op jit(solution)/shard_map/while/body/eval_jaxpr/ppermute | solution.py:10
  229.4 16.1 %collective-permute-start = (bf16[256,1024]{1,0:T(8,128)(2,1)S(1)}, bf16[256,1024]{1,0:T(8,128)(2,1)}, u32[]{:S(2)}, u32[]{:S(2)}) collective-permute-start(bf16[256,1024]{1,0:T(8,128)(2,1)S(1)} %get-tuple-element.67), channel_id=1, source_target_pairs={{240,0},{244,4},{248,8},{252,12},{0,16},{4,20},{8,24},{12,28},{16,... | collective-permute-start | bytes 1572872 | tf_op jit(solution)/shard_map/while/body/eval_jaxpr/ppermute | solution.py:10
  248.1 17.4 %collective-permute-start = (bf16[256,1024]{1,0:T(8,128)(2,1)S(1)}, bf16[256,1024]{1,0:T(8,128)(2,1)}, u32[]{:S(2)}, u32[]{:S(2)}) collective-permute-start(bf16[256,1024]{1,0:T(8,128)(2,1)S(1)} %get-tuple-element.67), channel_id=1, source_target_pairs={{240,0},{244,4},{248,8},{252,12},{0,16},{4,20},{8,24},{12,28},{16,... | collective-permute-start | bytes 1572872 | tf_op jit(solution)/shard_map/while/body/eval_jaxpr/ppermute | solution.py:10
  268.0 18.4 %collective-permute-start = (bf16[256,1024]{1,0:T(8,128)(2,1)S(1)}, bf16[256,1024]{1,0:T(8,128)(2,1)}, u32[]{:S(2)}, u32[]{:S(2)}) collective-permute-start(bf16[256,1024]{1,0:T(8,128)(2,1)S(1)} %get-tuple-element.67), channel_id=1, source_target_pairs={{240,0},{244,4},{248,8},{252,12},{0,16},{4,20},{8,24},{12,28},{16,... | collective-permute-start | bytes 1572872 | tf_op jit(solution)/shard_map/while/body/eval_jaxpr/ppermute | solution.py:10
  289.0 17.7 %collective-permute-start = (bf16[256,1024]{1,0:T(8,128)(2,1)S(1)}, bf16[256,1024]{1,0:T(8,128)(2,1)}, u32[]{:S(2)}, u32[]{:S(2)}) collective-permute-start(bf16[256,1024]{1,0:T(8,128)(2,1)S(1)} %get-tuple-element.67), channel_id=1, source_target_pairs={{240,0},{244,4},{248,8},{252,12},{0,16},{4,20},{8,24},{12,28},{16,... | collective-permute-start | bytes 1572872 | tf_op jit(solution)/shard_map/while/body/eval_jaxpr/ppermute | solution.py:10
  309.2 16.9 %collective-permute-start = (bf16[256,1024]{1,0:T(8,128)(2,1)S(1)}, bf16[256,1024]{1,0:T(8,128)(2,1)}, u32[]{:S(2)}, u32[]{:S(2)}) collective-permute-start(bf16[256,1024]{1,0:T(8,128)(2,1)S(1)} %get-tuple-element.67), channel_id=1, source_target_pairs={{240,0},{244,4},{248,8},{252,12},{0,16},{4,20},{8,24},{12,28},{16,... | collective-permute-start | bytes 1572872 | tf_op jit(solution)/shard_map/while/body/eval_jaxpr/ppermute | solution.py:10
  328.7 16.0 %collective-permute-start = (bf16[256,1024]{1,0:T(8,128)(2,1)S(1)}, bf16[256,1024]{1,0:T(8,128)(2,1)}, u32[]{:S(2)}, u32[]{:S(2)}) collective-permute-start(bf16[256,1024]{1,0:T(8,128)(2,1)S(1)} %get-tuple-element.67), channel_id=1, source_target_pairs={{240,0},{244,4},{248,8},{252,12},{0,16},{4,20},{8,24},{12,28},{16,... | collective-permute-start | bytes 1572872 | tf_op jit(solution)/shard_map/while/body/eval_jaxpr/ppermute | solution.py:10
  347.2 15.1 %collective-permute-start = (bf16[256,1024]{1,0:T(8,128)(2,1)S(1)}, bf16[256,1024]{1,0:T(8,128)(2,1)}, u32[]{:S(2)}, u32[]{:S(2)}) collective-permute-start(bf16[256,1024]{1,0:T(8,128)(2,1)S(1)} %get-tuple-element.67), channel_id=1, source_target_pairs={{240,0},{244,4},{248,8},{252,12},{0,16},{4,20},{8,24},{12,28},{16,... | collective-permute-start | bytes 1572872 | tf_op jit(solution)/shard_map/while/body/eval_jaxpr/ppermute | solution.py:10
  364.8 14.1 %collective-permute-start = (bf16[256,1024]{1,0:T(8,128)(2,1)S(1)}, bf16[256,1024]{1,0:T(8,128)(2,1)}, u32[]{:S(2)}, u32[]{:S(2)}) collective-permute-start(bf16[256,1024]{1,0:T(8,128)(2,1)S(1)} %get-tuple-element.67), channel_id=1, source_target_pairs={{240,0},{244,4},{248,8},{252,12},{0,16},{4,20},{8,24},{12,28},{16,... | collective-permute-start | bytes 1572872 | tf_op jit(solution)/shard_map/while/body/eval_jaxpr/ppermute | solution.py:10
  381.4 13.2 %collective-permute-start = (bf16[256,1024]{1,0:T(8,128)(2,1)S(1)}, bf16[256,1024]{1,0:T(8,128)(2,1)}, u32[]{:S(2)}, u32[]{:S(2)}) collective-permute-start(bf16[256,1024]{1,0:T(8,128)(2,1)S(1)} %get-tuple-element.67), channel_id=1, source_target_pairs={{240,0},{244,4},{248,8},{252,12},{0,16},{4,20},{8,24},{12,28},{16,... | collective-permute-start | bytes 1572872 | tf_op jit(solution)/shard_map/while/body/eval_jaxpr/ppermute | solution.py:10
  397.2 13.0 %collective-permute-start = (bf16[256,1024]{1,0:T(8,128)(2,1)S(1)}, bf16[256,1024]{1,0:T(8,128)(2,1)}, u32[]{:S(2)}, u32[]{:S(2)}) collective-permute-start(bf16[256,1024]{1,0:T(8,128)(2,1)S(1)} %get-tuple-element.67), channel_id=1, source_target_pairs={{240,0},{244,4},{248,8},{252,12},{0,16},{4,20},{8,24},{12,28},{16,... | collective-permute-start | bytes 1572872 | tf_op jit(solution)/shard_map/while/body/eval_jaxpr/ppermute | solution.py:10
  412.7 13.0 %collective-permute-start = (bf16[256,1024]{1,0:T(8,128)(2,1)S(1)}, bf16[256,1024]{1,0:T(8,128)(2,1)}, u32[]{:S(2)}, u32[]{:S(2)}) collective-permute-start(bf16[256,1024]{1,0:T(8,128)(2,1)S(1)} %get-tuple-element.67), channel_id=1, source_target_pairs={{240,0},{244,4},{248,8},{252,12},{0,16},{4,20},{8,24},{12,28},{16,... | collective-permute-start | bytes 1572872 | tf_op jit(solution)/shard_map/while/body/eval_jaxpr/ppermute | solution.py:10
  428.2 13.0 %collective-permute-start = (bf16[256,1024]{1,0:T(8,128)(2,1)S(1)}, bf16[256,1024]{1,0:T(8,128)(2,1)}, u32[]{:S(2)}, u32[]{:S(2)}) collective-permute-start(bf16[256,1024]{1,0:T(8,128)(2,1)S(1)} %get-tuple-element.67), channel_id=1, source_target_pairs={{240,0},{244,4},{248,8},{252,12},{0,16},{4,20},{8,24},{12,28},{16,... | collective-permute-start | bytes 1572872 | tf_op jit(solution)/shard_map/while/body/eval_jaxpr/ppermute | solution.py:10
  443.7 13.0 %collective-permute-start = (bf16[256,1024]{1,0:T(8,128)(2,1)S(1)}, bf16[256,1024]{1,0:T(8,128)(2,1)}, u32[]{:S(2)}, u32[]{:S(2)}) collective-permute-start(bf16[256,1024]{1,0:T(8,128)(2,1)S(1)} %get-tuple-element.67), channel_id=1, source_target_pairs={{240,0},{244,4},{248,8},{252,12},{0,16},{4,20},{8,24},{12,28},{16,... | collective-permute-start | bytes 1572872 | tf_op jit(solution)/shard_map/while/body/eval_jaxpr/ppermute | solution.py:10
  459.2 15.5 %copy-start.2 = (bf16[1,1024,1024]{2,1,0:T(8,128)(2,1)S(1)}, bf16[1,1024,1024]{2,1,0:T(8,128)(2,1)}, u32[]{:S(2)}) copy-start(bf16[1,1024,1024]{2,1,0:T(8,128)(2,1)} %param.5) | copy-start | bytes 6291460
  459.2 15.5 %copy-start.9 = (bf16[256,1024]{1,0:T(8,128)(2,1)S(1)}, bf16[256,1024]{1,0:T(8,128)(2,1)}, u32[]{:S(2)}) copy-start(bf16[256,1024]{1,0:T(8,128)(2,1)} %copy-done.8) | copy-start | bytes 1572868
  459.3 15.5 %copy-start.11 = (bf16[256,1024]{1,0:T(8,128)(2,1)S(1)}, bf16[256,1024]{1,0:T(8,128)(2,1)}, u32[]{:S(2)}) copy-start(bf16[256,1024]{1,0:T(8,128)(2,1)} %copy-done.10) | copy-start | bytes 1572868
  459.3 12.9 %collective-permute-start.5 = (bf16[256,1024]{1,0:T(8,128)(2,1)S(1)}, bf16[256,1024]{1,0:T(8,128)(2,1)S(1)}, u32[]{:S(2)}, u32[]{:S(2)}) collective-permute-start(bf16[256,1024]{1,0:T(8,128)(2,1)S(1)} %get-tuple-element.27), channel_id=1, source_target_pairs={{240,0},{244,4},{248,8},{252,12},{0,16},{4,20},{8,24},{12,28},{16,... | collective-permute-start | bytes 1572872 | tf_op jit(solution)/shard_map/ppermute | solution.py:10
Sparse Core Ops, SparseCore 0:
  62.1 33.9 all-gather.2
  150.9 36.3 all-gather.4
where the time goes:
time: 486 us; the launch traced here: 485 us
  waiting for transfers between devices  394 us (81%)
  matrix products  57.1 us (12%)
  between operations  13.6 us (3%)
  starting transfers between devices  13.5 us (3%)
    ppermute x16, waiting for transfers between devices, passed_along(): return lax.ppermute(block, axis, route)  232 us
    ppermute x4, waiting for transfers between devices, from_partner(): return lax.ppermute(block, axis, route)  128 us
    dot_general x19, matrix products, apply_map(): lax.dot_general(vectors, linear_map, (((1,), (1,)), ((), ())), preferred_...  45 us
    all_gather x2, waiting for transfers between devices, merge_level(): merged_map = lax.all_gather(row_block, 'face', axis=0, tiled=True)  34.1 us
    ppermute x16, starting transfers between devices, passed_along(): return lax.ppermute(block, axis, route)  11.6 us
  transfers between devices with their start and end apart: 22, of which 21 were waited for; matrix products, arithmetic and copies ran while one was open for 2% of the time, Pallas kernels for 0%

commit v1 on v0

v1 whole, which is shorter than its diff:
```python
import jax
import jax.numpy as jnp
from jax import lax
from jax.experimental import pallas as pl
from jax.experimental.pallas import tpu as pltpu
from jax.sharding import PartitionSpec as P

AXES = ("guide", "face")
BF16, F32 = jnp.bfloat16, jnp.float32


def coords(device):
    guide, face = divmod(device, 4)
    return guide // 2 % 4, guide % 2 * 2 + face // 2, guide // 8, face % 2


def device_at(x, y, z, core):
    x, y, z = x % 4, y % 4, z % 8
    return (z * 8 + x * 2 + y // 2) * 4 + y % 2 * 2 + core


def permute(block, target):
    route = [(i, device_at(*target(*coords(i)))) for i in range(256)]
    return lax.ppermute(block, AXES, route)


def to_core(x, y, z, c):
    return x, y, z, 1 - c


def to_y_mirror(x, y, z, c):
    return x, 3 - y, z, c


def to_y_pair(x, y, z, c):
    return x, y ^ 1, z, c


def to_y_next(x, y, z, c):
    return x, y + 1, z, c


def to_y_last(x, y, z, c):
    return x, y - 1, z, c


def to_y_far(x, y, z, c):
    return x, y + 2, z, c


def to_x_pair(x, y, z, c):
    return x ^ 1, y, z, c


def to_x_mirror(x, y, z, c):
    return 3 - x, y, z, c


def to_z_next(x, y, z, c):
    return x, y, z + 1, c


def rows_at(block, index, count):
    return lax.dynamic_slice_in_dim(block, index * count, count, 0)


def act(linear_map, vectors):
    return lax.dot_general(
        vectors, linear_map, (((1,), (1,)), ((), ())), preferred_element_type=F32
    )


def act_add(linear_map, vectors, added):
    return (act(linear_map, vectors) + added.astype(F32)).astype(BF16)


def merge_kernel(info, own, p0, p1, p2, p3, mine, theirs, product, other, trace):
    for slot, piece in enumerate((p0, p1, p2, p3)):
        start = pl.multiple_of(info[1 + slot] * 256, 256)
        other[pl.ds(start, 256), :] = piece[...]

    def merge(left, right, low, high):
        @pl.loop(0, 4)
        def _(tile):
            cols = pl.ds(pl.multiple_of(tile * 256, 256), 256)
            product[:, cols] = jnp.dot(
                left[...], right[:, cols], preferred_element_type=F32
            ).astype(BF16)

        trace[...] = act_add(left[...], low[...], high[...])

    @pl.when(info[0] == 1)
    def _():
        merge(own, other, theirs, mine)

    @pl.when(info[0] == 0)
    def _():
        merge(other, own, mine, theirs)


def merge(is_upper, order, own, pieces, mine, theirs):
    info = jnp.stack([is_upper] + order).astype(jnp.int32)
    full = pl.BlockSpec(memory_space=pltpu.VMEM)
    size = own.shape[0]
    return pl.pallas_call(
        merge_kernel,
        in_specs=[pl.BlockSpec(memory_space=pltpu.SMEM)] + [full] * 7,
        out_specs=[full] * 3,
        out_shape=[
            jax.ShapeDtypeStruct((size, size), BF16),
            jax.ShapeDtypeStruct((size, size), BF16),
            jax.ShapeDtypeStruct(mine.shape, BF16),
        ],
        compiler_params=pltpu.CompilerParams(vmem_limit_bytes=32 * 1024 * 1024),
        cost_estimate=pl.CostEstimate(
            flops=2 * size**3, bytes_accessed=8 * size**2, transcendentals=0
        ),
    )(info, own, *pieces, mine, theirs)


def local(transfer, leaf_map, volume_source):
    guide, face = lax.axis_index("guide"), lax.axis_index("face")
    x, y_hi, y_lo, core = guide // 2 % 4, guide % 2, face // 2, face % 2
    x_hi, x_lo = x // 2, x % 2
    strip = (x_lo + x_hi) % 2
    own_map = transfer[0]

    order = [face, face ^ 2, face ^ 1, face ^ 3]

    near = permute(rows_at(own_map, face ^ 2, 256), to_y_mirror)
    far = permute(near, to_y_pair)
    near_core, far_core = permute(near, to_core), permute(far, to_core)
    source = act(leaf_map[0], volume_source[0]).astype(BF16)
    theirs = permute(rows_at(source, 1 - y_hi, 128), to_y_far)
    source_rest = permute(rows_at(source, y_hi, 128), to_y_far)
    first_map, pair_map, first_trace = merge(
        y_hi, order, own_map, (near, far, near_core, far_core), rows_at(source, y_hi, 128), theirs
    )
    pair_trace = jnp.where(
        y_hi == 1,
        jnp.concatenate([source_rest, theirs], 0),
        jnp.concatenate([theirs, source_rest], 0),
    )

    def cross(block, partner):
        near = permute(rows_at(block, face, 256), partner)
        top = permute(near[:128], to_y_next)
        bottom = permute(near[128:], to_y_last)
        far = jnp.concatenate([top, bottom], 0)
        return near, far, permute(near, to_core), permute(far, to_core)

    pieces = cross(first_map, to_x_pair)
    theirs = permute(rows_at(first_trace, 1 - strip, 64), to_x_pair)
    rest = permute(rows_at(first_trace, strip, 64), to_x_pair)
    group_map, half_map, group_trace = merge(
        x_lo, order, first_map, pieces, rows_at(first_trace, strip, 64), theirs
    )
    half_trace = jnp.where(
        strip == 1, jnp.concatenate([rest, theirs], 0), jnp.concatenate([theirs, rest], 0)
    )
    half_trace_far = permute(half_trace, to_y_far)
    half_trace = jnp.where(
        y_hi == 1,
        jnp.concatenate([half_trace_far, half_trace], 0),
        jnp.concatenate([half_trace, half_trace_far], 0),
    )

    pieces = cross(group_map, to_x_mirror)
    theirs = permute(group_trace, to_x_mirror)
    plane_map, other_map, plane_trace = merge(
        x_hi, order, group_map, pieces, group_trace, theirs
    )

    moving = jnp.where(x_hi == 1, group_trace, plane_trace)
    for _ in range(7):
        moving = act_add(plane_map, permute(moving, to_z_next), plane_trace)
    arrived = permute(moving, to_z_next)
    entering = jnp.where(x_hi == 1, act_add(other_map, arrived, theirs), arrived)

    side = permute(entering, to_x_pair)
    half = jnp.where(
        strip == 1, jnp.concatenate([side, entering], 0), jnp.concatenate([entering, side], 0)
    )
    far = permute(half, to_y_far)
    entering = jnp.where(
        y_hi == 1, jnp.concatenate([far, half], 0), jnp.concatenate([half, far], 0)
    )
    lifted = jnp.where(x_lo == 1, act_add(half_map, entering, half_trace), entering)
    traces = jnp.where(y_hi == 1, act_add(pair_map, lifted, pair_trace), lifted)
    return traces[None]


def solution(mesh):
    in_specs = (P("guide", None, None), P("guide", None, None), P("guide", "face", None))
    out_specs = P("guide", "face", None)
    return jax.shard_map(local, mesh=mesh, in_specs=in_specs, out_specs=out_specs, check_vma=False)
```

time: 486 us -> 216 us (0.44)
  waiting for transfers between devices: 394 us -> 135 us
  matrix products: 57.1 us -> 19.2 us
  Pallas kernels: 0 us -> 16.2 us
  between operations: 13.6 us -> 0.24 us
  starting transfers between devices: 13.5 us -> 26.5 us
  local copies, waits for them, and re-layouts: 2.86 us -> 14.5 us
    ppermute x20 -> x30, waiting for transfers between devices: 360 us -> 135 us  [permute(): return lax.ppermute(block, AXES, route)]
    dot_general x22 -> x11, matrix products: 57.1 us -> 19.2 us  [act(): lax.dot_general(vectors, linear_map, (((1,), (1,)), ((), ())), preferred_...]
    all_gather x2 -> x0, waiting for transfers between devices: 34.1 us -> none  [merge_level(): merged_map = lax.all_gather(row_block, 'face', axis=0, tiled=True)]
    pallas_call x0 -> x3, Pallas kernels: none -> 16.2 us  [merge(): pl.pallas_call(merge_kernel, in_specs=[pl.BlockSpec(memory_space=pltpu.SM...]
    ppermute x20 -> x30, starting transfers between devices: 13.4 us -> 26.5 us  [permute(): return lax.ppermute(block, AXES, route)]
    unnamed x29 -> x32, local copies, waits for them, and re-layouts: 2.86 us -> 10.3 us
  transfers between devices with their start and end apart: 22 -> 30, of which waited for: 21 -> 22; matrix products, arithmetic and copies ran while one was open for 2% -> 7% of each run, Pallas kernels for 0% -> 0%
where the time goes in v1:
time: 216 us; the launch traced here: 212 us
  waiting for transfers between devices  135 us (62%)
  starting transfers between devices  26.5 us (12%)
  matrix products  19.2 us (9%)
  Pallas kernels  16.2 us (8%)
  local copies, waits for them, and re-layouts  14.5 us (7%)
    ppermute x30, waiting for transfers between devices, permute(): return lax.ppermute(block, AXES, route)  135 us
    ppermute x30, starting transfers between devices, permute(): return lax.ppermute(block, AXES, route)  26.5 us
    dot_general x11, matrix products, act(): lax.dot_general(vectors, linear_map, (((1,), (1,)), ((), ())), preferred_...  19.2 us
    pallas_call x3, Pallas kernels, merge(): pl.pallas_call(merge_kernel, in_specs=[pl.BlockSpec(memory_space=pltpu.SM...  16.2 us
    unnamed x32, local copies, waits for them, and re-layouts  10.3 us
  transfers between devices with their start and end apart: 30, of which 22 were waited for; matrix products, arithmetic and copies ran while one was open for 7% of the time, Pallas kernels for 0%

profile of v1, /device:TPU:18, one launch (start us, length us, event | category | flops | bytes accessed | tf_op | source)
XLA Modules:
  0.0 211.8 jit_solution(3092939203354269742)
XLA Ops:
  0.0 1.2 dynamic-slice_bitcast_fusion
  1.2 0.5 collective-permute-start
  1.8 13.2 %collective-permute-done.p0 = bf16[256,1024]{1,0:T(8,128)(2,1)S(1)} collective-permute-done((bf16[256,1024]{1,0:T(8,128)(2,1)S(1)}, bf16[256,1024]{1,0:T(8,128)(2,1)S(1)}, u32[]{:S(2)}, u32[]{:S(2)}) %collective-permute-start) | collective-permute-done | bytes 524320 | tf_op jit(solution)/shard_map/ppermute | solution.py:24
  15.0 2.5 %collective-permute-start.1 = (bf16[256,1024]{1,0:T(8,128)(2,1)S(1)}, bf16[256,1024]{1,0:T(8,128)(2,1)S(1)}, u32[]{:S(2)}, u32[]{:S(2)}) collective-permute-start(bf16[256,1024]{1,0:T(8,128)(2,1)S(1)} %collective-permute-done.p0), channel_id=1, source_target_pairs={{0,2},{1,3},{2,0},{3,1},{4,6},{5,7},{6,4},{7,5},{8,10},{9,11},{10,... | collective-permute-start | bytes 1572872 | tf_op jit(solution)/shard_map/ppermute | solution.py:24
  17.5 11.0 %collective-permute-done.1.p1 = bf16[256,1024]{1,0:T(8,128)(2,1)S(1)} collective-permute-done((bf16[256,1024]{1,0:T(8,128)(2,1)S(1)}, bf16[256,1024]{1,0:T(8,128)(2,1)S(1)}, u32[]{:S(2)}, u32[]{:S(2)}) %collective-permute-start.1) | collective-permute-done | bytes 524320 | tf_op jit(solution)/shard_map/ppermute | solution.py:24
  28.5 6.7 %fusion.3 = bf16[256,1024]{1,0:T(8,128)(2,1)} fusion(bf16[1,1024,4096]{2,1,0:T(8,128)(2,1)} %param.4, bf16[1,256,4096]{2,1,0:T(8,128)(2,1)S(1)} %copy-done), kind=kOutput, calls=%fused_computation.5 | convolution fusion | flops 2147745792 | bytes 11010048 | tf_op jit(solution)/shard_map/dot_general | solution.py:68
  35.3 1.8 constant_dynamic-slice_fusion.4
  37.1 0.9 collective-permute-start.4
  38.1 9.3 %collective-permute-done.4.theirs = bf16[128,1024]{1,0:T(8,128)(2,1)} collective-permute-done((bf16[128,1024]{1,0:T(8,128)(2,1)}, bf16[128,1024]{1,0:T(8,128)(2,1)}, u32[]{:S(2)}, u32[]{:S(2)}) %collective-permute-start.4) | collective-permute-done | bytes 262176 | tf_op jit(solution)/shard_map/ppermute | solution.py:24
  47.4 1.6 copy-done.1
  49.0 1.0 copy-done.9
  50.1 1.0 copy-done.11
  51.1 5.1 %shard_map.37 = (bf16[1024,1024]{1,0:T(8,128)(2,1)S(1)}, bf16[1024,1024]{1,0:T(8,128)(2,1)S(1)}, bf16[128,1024]{1,0:T(8,128)(2,1)S(1)}) custom-call(s32[5]{0:T(128)S(1)} %stack.45.info, bf16[1024,1024]{1,0:T(8,128)(2,1)S(1)} %bitcast.41, bf16[256,1024]{1,0:T(8,128)(2,1)S(1)} %copy-done.9, bf16[256,1024]{1,0:T(8,128)(2,1)S(1)} %copy-done.11, ...), custom_call_target="tpu_custom_call" | custom-call | flops 2147483648 | bytes 8388608 | tf_op jit(solution)/shard_map/pallas_call | solution.py:105
  56.2 1.3 copy-done.12
  57.6 0.6 collective-permute-start.5
  58.2 12.8 %collective-permute-done.5.p0 = bf16[256,1024]{1,0:T(8,128)(2,1)S(1)} collective-permute-done((bf16[256,1024]{1,0:T(8,128)(2,1)S(1)}, bf16[256,1024]{1,0:T(8,128)(2,1)S(1)}, u32[]{:S(2)}, u32[]{:S(2)}) %collective-permute-start.5) | collective-permute-done | bytes 524320 | tf_op jit(solution)/shard_map/ppermute | solution.py:24
  71.1 1.8 collective-permute-start.6
  73.2 4.8 %collective-permute-done.6 = bf16[128,1024]{1,0:T(8,128)(2,1)S(1)} collective-permute-done((bf16[128,1024]{1,0:T(8,128)(2,1)S(1)}, bf16[128,1024]{1,0:T(8,128)(2,1)S(1)}, u32[]{:S(2)}, u32[]{:S(2)}) %collective-permute-start.6) | collective-permute-done | bytes 262176 | tf_op jit(solution)/shard_map/ppermute | solution.py:24
  78.0 0.7 constant_dynamic-update-slice_fusion.1
  78.7 0.7 collective-permute-done.7
  79.4 0.7 constant_dynamic-update-slice_fusion.p1
  80.2 0.6 collective-permute-start.10
  80.9 5.3 %collective-permute-done.10.theirs = bf16[64,1024]{1,0:T(8,128)(2,1)S(1)} collective-permute-done((bf16[64,1024]{1,0:T(8,128)(2,1)S(1)}, bf16[64,1024]{1,0:T(8,128)(2,1)S(1)}, u32[]{:S(2)}, u32[]{:S(2)}) %collective-permute-start.10) | collective-permute-done | bytes 131104 | tf_op jit(solution)/shard_map/ppermute | solution.py:24
  86.2 1.6 copy-done.3
  87.8 6.0 %shard_map.38 = (bf16[1024,1024]{1,0:T(8,128)(2,1)S(1)}, bf16[1024,1024]{1,0:T(8,128)(2,1)S(1)}, bf16[64,1024]{1,0:T(8,128)(2,1)}) custom-call(s32[5]{0:T(128)S(1)} %stack.43.info, bf16[1024,1024]{1,0:T(8,128)(2,1)S(1)} %copy-done.3, bf16[256,1024]{1,0:T(8,128)(2,1)S(1)} %collective-permute-done.5.p0, ...), custom_call_target="tpu_custom_call" | custom-call | flops 2147483648 | bytes 8388608 | tf_op jit(solution)/shard_map/pallas_call | solution.py:105
  93.8 1.3 copy-done.14
  95.1 1.6 collective-permute-start.11
  96.7 12.1 %collective-permute-done.11.p0 = bf16[256,1024]{1,0:T(8,128)(2,1)S(1)} collective-permute-done((bf16[256,1024]{1,0:T(8,128)(2,1)S(1)}, bf16[256,1024]{1,0:T(8,128)(2,1)S(1)}, u32[]{:S(2)}, u32[]{:S(2)}) %collective-permute-start.11) | collective-permute-done | bytes 524320 | tf_op jit(solution)/shard_map/ppermute | solution.py:24
  108.8 1.7 collective-permute-start.12
  110.5 0.4 collective-permute-start.13
  110.9 5.0 %collective-permute-done.12 = bf16[128,1024]{1,0:T(8,128)(2,1)S(1)} collective-permute-done((bf16[128,1024]{1,0:T(8,128)(2,1)S(1)}, bf16[128,1024]{1,0:T(8,128)(2,1)S(1)}, u32[]{:S(2)}, u32[]{:S(2)}) %collective-permute-start.12) | collective-permute-done | bytes 262176 | tf_op jit(solution)/shard_map/ppermute | solution.py:24
  116.0 1.3 collective-permute-done.13
  117.4 1.6 collective-permute-start.16
  119.0 4.6 %collective-permute-done.16.theirs = bf16[64,1024]{1,0:T(8,128)(2,1)} collective-permute-done((bf16[64,1024]{1,0:T(8,128)(2,1)}, bf16[64,1024]{1,0:T(8,128)(2,1)}, u32[]{:S(2)}, u32[]{:S(2)}) %collective-permute-start.16) | collective-permute-done | bytes 131104 | tf_op jit(solution)/shard_map/ppermute | solution.py:24
  123.6 1.6 copy-done.5
  125.2 5.1 %shard_map.39 = (bf16[1024,1024]{1,0:T(8,128)(2,1)S(1)}, bf16[1024,1024]{1,0:T(8,128)(2,1)S(1)}, bf16[64,1024]{1,0:T(8,128)(2,1)S(1)}) custom-call(s32[5]{0:T(128)S(1)} %stack.47.info, bf16[1024,1024]{1,0:T(8,128)(2,1)S(1)} %copy-done.5, bf16[256,1024]{1,0:T(8,128)(2,1)S(1)} %collective-permute-done.11.p0, ...), custom_call_target="tpu_custom_call" | custom-call | flops 2147483648 | bytes 8388608 | tf_op jit(solution)/shard_map/pallas_call | solution.py:105
  130.3 2.0 collective-permute-start.17
  132.3 7.3 %collective-permute-done.17 = bf16[64,1024]{1,0:T(8,128)(2,1)S(1)} collective-permute-done((bf16[64,1024]{1,0:T(8,128)(2,1)S(1)}, bf16[64,1024]{1,0:T(8,128)(2,1)S(1)}, u32[]{:S(2)}, u32[]{:S(2)}) %collective-permute-start.17) | collective-permute-done | bytes 131104 | tf_op jit(solution)/shard_map/ppermute | solution.py:24
  139.5 0.8 fusion.13
  140.4 6.2 %collective-permute-done.18 = bf16[64,1024]{1,0:T(8,128)(2,1)S(1)} collective-permute-done((bf16[64,1024]{1,0:T(8,128)(2,1)S(1)}, bf16[64,1024]{1,0:T(8,128)(2,1)S(1)}, u32[]{:S(2)}, u32[]{:S(2)}) %collective-permute-start.18) | collective-permute-done | bytes 131104 | tf_op jit(solution)/shard_map/ppermute | solution.py:24
  146.6 0.8 fusion.14
  147.4 6.2 %collective-permute-done.19 = bf16[64,1024]{1,0:T(8,128)(2,1)S(1)} collective-permute-done((bf16[64,1024]{1,0:T(8,128)(2,1)S(1)}, bf16[64,1024]{1,0:T(8,128)(2,1)S(1)}, u32[]{:S(2)}, u32[]{:S(2)}) %collective-permute-start.19) | collective-permute-done | bytes 131104 | tf_op jit(solution)/shard_map/ppermute | solution.py:24
  153.6 0.8 fusion.15
  154.3 0.3 collective-permute-start.20
  154.6 6.2 %collective-permute-done.20 = bf16[64,1024]{1,0:T(8,128)(2,1)S(1)} collective-permute-done((bf16[64,1024]{1,0:T(8,128)(2,1)S(1)}, bf16[64,1024]{1,0:T(8,128)(2,1)S(1)}, u32[]{:S(2)}, u32[]{:S(2)}) %collective-permute-start.20) | collective-permute-done | bytes 131104 | tf_op jit(solution)/shard_map/ppermute | solution.py:24
  160.8 0.8 fusion.16
  161.6 7.1 %collective-permute-done.21 = bf16[64,1024]{1,0:T(8,128)(2,1)S(1)} collective-permute-done((bf16[64,1024]{1,0:T(8,128)(2,1)S(1)}, bf16[64,1024]{1,0:T(8,128)(2,1)S(1)}, u32[]{:S(2)}, u32[]{:S(2)}) %collective-permute-start.21) | collective-permute-done | bytes 131104 | tf_op jit(solution)/shard_map/ppermute | solution.py:24
  168.8 0.8 fusion.17
  169.6 6.9 %collective-permute-done.22 = bf16[64,1024]{1,0:T(8,128)(2,1)S(1)} collective-permute-done((bf16[64,1024]{1,0:T(8,128)(2,1)S(1)}, bf16[64,1024]{1,0:T(8,128)(2,1)S(1)}, u32[]{:S(2)}, u32[]{:S(2)}) %collective-permute-start.22) | collective-permute-done | bytes 131104 | tf_op jit(solution)/shard_map/ppermute | solution.py:24
  176.5 0.8 fusion.18
  177.3 6.2 %collective-permute-done.23 = bf16[64,1024]{1,0:T(8,128)(2,1)S(1)} collective-permute-done((bf16[64,1024]{1,0:T(8,128)(2,1)S(1)}, bf16[64,1024]{1,0:T(8,128)(2,1)S(1)}, u32[]{:S(2)}, u32[]{:S(2)}) %collective-permute-start.23) | collective-permute-done | bytes 131104 | tf_op jit(solution)/shard_map/ppermute | solution.py:24
  183.5 0.8 fusion.19
  184.4 3.0 %collective-permute-start.27 = (bf16[64,1024]{1,0:T(8,128)(2,1)S(1)}, bf16[64,1024]{1,0:T(8,128)(2,1)S(1)}, u32[]{:S(2)}, u32[]{:S(2)}) collective-permute-start(bf16[64,1024]{1,0:T(8,128)(2,1)S(1)} %copy-done.7), channel_id=1, source_target_pairs={{0,8},{1,9},{2,10},{3,11},{4,12},{5,13},{6,14},{7,15},{8,0},{9,1},... | collective-permute-start | bytes 393224 | tf_op jit(solution)/shard_map/ppermute | solution.py:24
  187.4 3.1 %collective-permute-done.24 = bf16[64,1024]{1,0:T(8,128)(2,1)S(1)} collective-permute-done((bf16[64,1024]{1,0:T(8,128)(2,1)S(1)}, bf16[64,1024]{1,0:T(8,128)(2,1)S(1)}, u32[]{:S(2)}, u32[]{:S(2)}) %collective-permute-start.24) | collective-permute-done | bytes 131104 | tf_op jit(solution)/shard_map/ppermute | solution.py:24
  190.5 1.7 fusion.21
  192.2 3.0 %collective-permute-start.25 = (bf16[64,1024]{1,0:T(8,128)(2,1)S(1)}, bf16[64,1024]{1,0:T(8,128)(2,1)S(1)}, u32[]{:S(2)}, u32[]{:S(2)}) collective-permute-start(bf16[64,1024]{1,0:T(8,128)(2,1)S(1)} %fusion.21), channel_id=1, source_target_pairs={{0,8},{1,9},{2,10},{3,11},{4,12},{5,13},{6,14},{7,15},{8,0},{9,1},... | collective-permute-start | bytes 393224 | tf_op jit(solution)/shard_map/ppermute | solution.py:24
  195.3 1.4 collective-permute-start.28
  196.7 1.5 collective-permute-done.25
  198.2 1.4 collective-permute-start.26
  199.6 2.2 %collective-permute-start.29 = (bf16[128,1024]{1,0:T(8,128)(2,1)S(1)}, bf16[128,1024]{1,0:T(8,128)(2,1)S(1)}, u32[]{:S(2)}, u32[]{:S(2)}) collective-permute-start(bf16[128,1024]{1,0:T(8,128)(2,1)S(1)} %get-tuple-element.28.mine), channel_id=1, source_target_pairs={{0,4},{1,5},{2,6},{3,7},{4,0},{5,1},{6,2},{7,3},{8,12},{9,13},{10,... | collective-permute-start | bytes 786440 | tf_op jit(solution)/shard_map/ppermute | solution.py:24
  201.8 1.4 collective-permute-done.28
  203.2 3.0 %collective-permute-done.26 = bf16[128,1024]{1,0:T(8,128)(2,1)} collective-permute-done((bf16[128,1024]{1,0:T(8,128)(2,1)S(1)}, bf16[128,1024]{1,0:T(8,128)(2,1)}, u32[]{:S(2)}, u32[]{:S(2)}) %collective-permute-start.26) | collective-permute-done | bytes 262176 | tf_op jit(solution)/shard_map/ppermute | solution.py:24
  206.3 2.8 %fusion.9 = bf16[256,1024]{1,0:T(8,128)(2,1)S(1)} fusion(bf16[1024,1024]{1,0:T(8,128)(2,1)} %copy-done.14, bf16[128,1024]{1,0:T(8,128)(2,1)S(1)} %maximum_select_fusion.4, bf16[128,1024]{1,0:T(8,128)(2,1)} %collective-permute-done.26, bf16[128,1024]{1,0:T(8,128)(2,1)S(1)} %maximum_select_fusion.5, bf16[128,1024]{1,0:T(8,128)(2,1)S(1)} %collective-permute-done.28, ...), kind=kOutput, calls=%fused_computation.7 | convolution fusion | flops 544997376 | bytes 3670018 | tf_op jit(solution)/shard_map/dot_general | solution.py:68
  209.1 2.7 %fusion.12 = bf16[1,256,1024]{2,1,0:T(8,128)(2,1)} fusion(bf16[256,1024]{1,0:T(8,128)(2,1)S(1)} %fusion.9, bf16[1024,1024]{1,0:T(8,128)(2,1)S(1)} %copy-done.13, bf16[128,1024]{1,0:T(8,128)(2,1)} %collective-permute-done.4.theirs, bf16[128,1024]{1,0:T(8,128)(2,1)S(1)} %collective-permute-done.29, pred[]{:T(512)S(6)} %eq.22), kind=kOutput, calls=%fused_computation.10 | convolution fusion | flops 540278784 | bytes 3670017 | tf_op jit(solution)/shard_map/dot_general | solution.py:68
  (57 shorter events, 1.5 us)
Async XLA Ops:
  0.0 28.5 %copy-start = (bf16[1,256,4096]{2,1,0:T(8,128)(2,1)S(1)}, bf16[1,256,4096]{2,1,0:T(8,128)(2,1)}, u32[]{:S(2)}) copy-start(bf16[1,256,4096]{2,1,0:T(8,128)(2,1)} %param.5) | copy-start | bytes 6291460
  1.2 13.8 %collective-permute-start = (bf16[256,1024]{1,0:T(8,128)(2,1)S(1)}, bf16[256,1024]{1,0:T(8,128)(2,1)S(1)}, u32[]{:S(2)}, u32[]{:S(2)}) collective-permute-start(bf16[256,1024]{1,0:T(8,128)(2,1)S(1)} %dynamic-slice_bitcast_fusion), channel_id=1, source_target_pairs={{0,6},{1,7},{2,4},{3,5},{4,2},{5,3},{6,0},{7,1},{8,14},{9,15},{10,... | collective-permute-start | bytes 1572872 | tf_op jit(solution)/shard_map/ppermute | solution.py:24
  15.0 20.3 %copy-start.8 = (bf16[256,1024]{1,0:T(8,128)(2,1)}, bf16[256,1024]{1,0:T(8,128)(2,1)S(1)}, u32[]{:S(2)}) copy-start(bf16[256,1024]{1,0:T(8,128)(2,1)S(1)} %collective-permute-done.p0) | copy-start | bytes 1572868
  15.0 13.5 %collective-permute-start.1 = (bf16[256,1024]{1,0:T(8,128)(2,1)S(1)}, bf16[256,1024]{1,0:T(8,128)(2,1)S(1)}, u32[]{:S(2)}, u32[]{:S(2)}) collective-permute-start(bf16[256,1024]{1,0:T(8,128)(2,1)S(1)} %collective-permute-done.p0), channel_id=1, source_target_pairs={{0,2},{1,3},{2,0},{3,1},{4,6},{5,7},{6,4},{7,5},{8,10},{9,11},{10,... | collective-permute-start | bytes 1572872 | tf_op jit(solution)/shard_map/ppermute | solution.py:24
  17.5 29.9 %collective-permute-start.2 = (bf16[256,1024]{1,0:T(8,128)(2,1)S(1)}, bf16[256,1024]{1,0:T(8,128)(2,1)}, u32[]{:S(2)}, u32[]{:S(2)}) collective-permute-start(bf16[256,1024]{1,0:T(8,128)(2,1)S(1)} %collective-permute-done.p0), channel_id=1, source_target_pairs={{0,1},{1,0},{2,3},{3,2},{4,5},{5,4},{6,7},{7,6},{8,9},{9,8},{10,11... | collective-permute-start | bytes 1572872 | tf_op jit(solution)/shard_map/ppermute | solution.py:24
  28.5 6.7 %copy-start.10 = (bf16[256,1024]{1,0:T(8,128)(2,1)}, bf16[256,1024]{1,0:T(8,128)(2,1)S(1)}, u32[]{:S(2)}) copy-start(bf16[256,1024]{1,0:T(8,128)(2,1)S(1)} %collective-permute-done.1.p1) | copy-start | bytes 1572868
  28.5 18.9 %collective-permute-start.3 = (bf16[256,1024]{1,0:T(8,128)(2,1)S(1)}, bf16[256,1024]{1,0:T(8,128)(2,1)}, u32[]{:S(2)}, u32[]{:S(2)}) collective-permute-start(bf16[256,1024]{1,0:T(8,128)(2,1)S(1)} %collective-permute-done.1.p1), channel_id=1, source_target_pairs={{0,1},{1,0},{2,3},{3,2},{4,5},{5,4},{6,7},{7,6},{8,9},{9,8},{10,11... | collective-permute-start | bytes 1572872 | tf_op jit(solution)/shard_map/ppermute | solution.py:24
  37.1 10.3 %collective-permute-start.4 = (bf16[128,1024]{1,0:T(8,128)(2,1)}, bf16[128,1024]{1,0:T(8,128)(2,1)}, u32[]{:S(2)}, u32[]{:S(2)}) collective-permute-start(bf16[128,1024]{1,0:T(8,128)(2,1)} %get-tuple-element.27), channel_id=1, source_target_pairs={{0,4},{1,5},{2,6},{3,7},{4,0},{5,1},{6,2},{7,3},{8,12},{9,13},{10,... | collective-permute-start | bytes 786440 | tf_op jit(solution)/shard_map/ppermute | solution.py:24
  47.4 1.6 copy-start.1
  49.0 1.0 copy-start.9
  50.1 1.0 copy-start.11
  56.2 1.3 copy-start.12
  57.6 15.3 %copy-start.2 = (bf16[1024,1024]{1,0:T(8,128)(2,1)}, bf16[1024,1024]{1,0:T(8,128)(2,1)S(1)}, u32[]{:S(2)}) copy-start(bf16[1024,1024]{1,0:T(8,128)(2,1)S(1)} %get-tuple-element.14.own) | copy-start | bytes 6291460
  57.6 13.4 %collective-permute-start.5 = (bf16[256,1024]{1,0:T(8,128)(2,1)S(1)}, bf16[256,1024]{1,0:T(8,128)(2,1)S(1)}, u32[]{:S(2)}, u32[]{:S(2)}) collective-permute-start(bf16[256,1024]{1,0:T(8,128)(2,1)S(1)} %constant_dynamic-slice_fusion.3), channel_id=1, source_target_pairs={{0,8},{1,9},{2,10},{3,11},{4,12},{5,13},{6,14},{7,15},{8,0},{9,1},... | collective-permute-start | bytes 1572872 | tf_op jit(solution)/shard_map/ppermute | solution.py:24
  71.1 6.9 %collective-permute-start.6 = (bf16[128,1024]{1,0:T(8,128)(2,1)S(1)}, bf16[128,1024]{1,0:T(8,128)(2,1)S(1)}, u32[]{:S(2)}, u32[]{:S(2)}) collective-permute-start(bf16[128,1024]{1,0:T(8,128)(2,1)S(1)} %get-tuple-element.26), channel_id=1, source_target_pairs={{0,2},{1,3},{2,4},{3,5},{4,6},{5,7},{6,0},{7,1},{8,10},{9,11},{10,... | collective-permute-start | bytes 786440 | tf_op jit(solution)/shard_map/ppermute | solution.py:24
  72.9 6.5 %collective-permute-start.7 = (bf16[128,1024]{1,0:T(8,128)(2,1)S(1)}, bf16[128,1024]{1,0:T(8,128)(2,1)S(1)}, u32[]{:S(2)}, u32[]{:S(2)}) collective-permute-start(bf16[128,1024]{1,0:T(8,128)(2,1)S(1)} %get-tuple-element.25), channel_id=1, source_target_pairs={{0,6},{1,7},{2,0},{3,1},{4,2},{5,3},{6,4},{7,5},{8,14},{9,15},{10,... | collective-permute-start | bytes 786440 | tf_op jit(solution)/shard_map/ppermute | solution.py:24
  73.2 13.0 %collective-permute-start.8 = (bf16[256,1024]{1,0:T(8,128)(2,1)S(1)}, bf16[256,1024]{1,0:T(8,128)(2,1)}, u32[]{:S(2)}, u32[]{:S(2)}) collective-permute-start(bf16[256,1024]{1,0:T(8,128)(2,1)S(1)} %collective-permute-done.5.p0), channel_id=1, source_target_pairs={{0,1},{1,0},{2,3},{3,2},{4,5},{5,4},{6,7},{7,6},{8,9},{9,8},{10,11... | collective-permute-start | bytes 1572872 | tf_op jit(solution)/shard_map/ppermute | solution.py:24
  80.1 6.0 %collective-permute-start.9 = (bf16[256,1024]{1,0:T(8,128)(2,1)}, bf16[256,1024]{1,0:T(8,128)(2,1)}, u32[]{:S(2)}, u32[]{:S(2)}) collective-permute-start(bf16[256,1024]{1,0:T(8,128)(2,1)} %constant_dynamic-update-slice_fusion.p1), channel_id=1, source_target_pairs={{0,1},{1,0},{2,3},{3,2},{4,5},{5,4},{6,7},{7,6},{8,9},{9,8},{10,11... | collective-permute-start | bytes 1572872 | tf_op jit(solution)/shard_map/ppermute | solution.py:24
  80.2 13.6 %copy-start.6 = (bf16[64,1024]{1,0:T(8,128)(2,1)}, bf16[64,1024]{1,0:T(8,128)(2,1)S(1)}, u32[]{:S(2)}) copy-start(bf16[64,1024]{1,0:T(8,128)(2,1)S(1)} %get-tuple-element.30.mine) | copy-start | bytes 393220
  80.2 6.0 %collective-permute-start.10 = (bf16[64,1024]{1,0:T(8,128)(2,1)S(1)}, bf16[64,1024]{1,0:T(8,128)(2,1)S(1)}, u32[]{:S(2)}, u32[]{:S(2)}) collective-permute-start(bf16[64,1024]{1,0:T(8,128)(2,1)S(1)} %get-tuple-element.29), channel_id=1, source_target_pairs={{0,8},{1,9},{2,10},{3,11},{4,12},{5,13},{6,14},{7,15},{8,0},{9,1},... | collective-permute-start | bytes 393224 | tf_op jit(solution)/shard_map/ppermute | solution.py:24
  86.2 1.6 copy-start.3
  93.8 1.3 copy-start.14
  95.1 22.2 %copy-start.4 = (bf16[1024,1024]{1,0:T(8,128)(2,1)}, bf16[1024,1024]{1,0:T(8,128)(2,1)S(1)}, u32[]{:S(2)}) copy-start(bf16[1024,1024]{1,0:T(8,128)(2,1)S(1)} %get-tuple-element.17.own) | copy-start | bytes 6291460
  95.1 13.6 %collective-permute-start.11 = (bf16[256,1024]{1,0:T(8,128)(2,1)S(1)}, bf16[256,1024]{1,0:T(8,128)(2,1)S(1)}, u32[]{:S(2)}, u32[]{:S(2)}) collective-permute-start(bf16[256,1024]{1,0:T(8,128)(2,1)S(1)} %constant_dynamic-slice_fusion), channel_id=1, source_target_pairs={{0,24},{1,25},{2,26},{3,27},{4,28},{5,29},{6,30},{7,31},{8,16},{9,... | collective-permute-start | bytes 1572872 | tf_op jit(solution)/shard_map/ppermute | solution.py:24
  108.8 7.1 %collective-permute-start.12 = (bf16[128,1024]{1,0:T(8,128)(2,1)S(1)}, bf16[128,1024]{1,0:T(8,128)(2,1)S(1)}, u32[]{:S(2)}, u32[]{:S(2)}) collective-permute-start(bf16[128,1024]{1,0:T(8,128)(2,1)S(1)} %get-tuple-element.24), channel_id=1, source_target_pairs={{0,2},{1,3},{2,4},{3,5},{4,6},{5,7},{6,0},{7,1},{8,10},{9,11},{10,... | collective-permute-start | bytes 786440 | tf_op jit(solution)/shard_map/ppermute | solution.py:24
  110.5 6.8 %collective-permute-start.13 = (bf16[128,1024]{1,0:T(8,128)(2,1)S(1)}, bf16[128,1024]{1,0:T(8,128)(2,1)S(1)}, u32[]{:S(2)}, u32[]{:S(2)}) collective-permute-start(bf16[128,1024]{1,0:T(8,128)(2,1)S(1)} %get-tuple-element.23), channel_id=1, source_target_pairs={{0,6},{1,7},{2,0},{3,1},{4,2},{5,3},{6,4},{7,5},{8,14},{9,15},{10,... | collective-permute-start | bytes 786440 | tf_op jit(solution)/shard_map/ppermute | solution.py:24
  110.9 12.7 %collective-permute-start.14 = (bf16[256,1024]{1,0:T(8,128)(2,1)S(1)}, bf16[256,1024]{1,0:T(8,128)(2,1)}, u32[]{:S(2)}, u32[]{:S(2)}) collective-permute-start(bf16[256,1024]{1,0:T(8,128)(2,1)S(1)} %collective-permute-done.11.p0), channel_id=1, source_target_pairs={{0,1},{1,0},{2,3},{3,2},{4,5},{5,4},{6,7},{7,6},{8,9},{9,8},{10,11... | collective-permute-start | bytes 1572872 | tf_op jit(solution)/shard_map/ppermute | solution.py:24
  117.3 6.3 %collective-permute-start.15 = (bf16[256,1024]{1,0:T(8,128)(2,1)S(1)}, bf16[256,1024]{1,0:T(8,128)(2,1)}, u32[]{:S(2)}, u32[]{:S(2)}) collective-permute-start(bf16[256,1024]{1,0:T(8,128)(2,1)S(1)} %constant_dynamic-update-slice_fusion.2.p1), channel_id=1, source_target_pairs={{0,1},{1,0},{2,3},{3,2},{4,5},{5,4},{6,7},{7,6},{8,9},{9,8},{10,11... | collective-permute-start | bytes 1572872 | tf_op jit(solution)/shard_map/ppermute | solution.py:24
  117.4 6.2 %collective-permute-start.16 = (bf16[64,1024]{1,0:T(8,128)(2,1)}, bf16[64,1024]{1,0:T(8,128)(2,1)}, u32[]{:S(2)}, u32[]{:S(2)}) collective-permute-start(bf16[64,1024]{1,0:T(8,128)(2,1)} %get-tuple-element.16.mine), channel_id=1, source_target_pairs={{0,24},{1,25},{2,26},{3,27},{4,28},{5,29},{6,30},{7,31},{8,16},{9,... | collective-permute-start | bytes 393224 | tf_op jit(solution)/shard_map/ppermute | solution.py:24
  123.6 1.6 copy-start.5
  130.3 9.2 %collective-permute-start.17 = (bf16[64,1024]{1,0:T(8,128)(2,1)S(1)}, bf16[64,1024]{1,0:T(8,128)(2,1)S(1)}, u32[]{:S(2)}, u32[]{:S(2)}) collective-permute-start(bf16[64,1024]{1,0:T(8,128)(2,1)S(1)} %broadcast_select_fusion), channel_id=1, source_target_pairs={{0,32},{1,33},{2,34},{3,35},{4,36},{5,37},{6,38},{7,39},{8,40},{9,... | collective-permute-start | bytes 393224 | tf_op jit(solution)/shard_map/ppermute | solution.py:24
  140.3 6.3 %collective-permute-start.18 = (bf16[64,1024]{1,0:T(8,128)(2,1)S(1)}, bf16[64,1024]{1,0:T(8,128)(2,1)S(1)}, u32[]{:S(2)}, u32[]{:S(2)}) collective-permute-start(bf16[64,1024]{1,0:T(8,128)(2,1)S(1)} %fusion.13), channel_id=1, source_target_pairs={{0,32},{1,33},{2,34},{3,35},{4,36},{5,37},{6,38},{7,39},{8,40},{9,... | collective-permute-start | bytes 393224 | tf_op jit(solution)/shard_map/ppermute | solution.py:24
  147.3 6.3 %collective-permute-start.19 = (bf16[64,1024]{1,0:T(8,128)(2,1)S(1)}, bf16[64,1024]{1,0:T(8,128)(2,1)S(1)}, u32[]{:S(2)}, u32[]{:S(2)}) collective-permute-start(bf16[64,1024]{1,0:T(8,128)(2,1)S(1)} %fusion.14), channel_id=1, source_target_pairs={{0,32},{1,33},{2,34},{3,35},{4,36},{5,37},{6,38},{7,39},{8,40},{9,... | collective-permute-start | bytes 393224 | tf_op jit(solution)/shard_map/ppermute | solution.py:24
  154.3 6.5 %collective-permute-start.20 = (bf16[64,1024]{1,0:T(8,128)(2,1)S(1)}, bf16[64,1024]{1,0:T(8,128)(2,1)S(1)}, u32[]{:S(2)}, u32[]{:S(2)}) collective-permute-start(bf16[64,1024]{1,0:T(8,128)(2,1)S(1)} %fusion.15), channel_id=1, source_target_pairs={{0,32},{1,33},{2,34},{3,35},{4,36},{5,37},{6,38},{7,39},{8,40},{9,... | collective-permute-start | bytes 393224 | tf_op jit(solution)/shard_map/ppermute | solution.py:24
  161.6 7.2 %collective-permute-start.21 = (bf16[64,1024]{1,0:T(8,128)(2,1)S(1)}, bf16[64,1024]{1,0:T(8,128)(2,1)S(1)}, u32[]{:S(2)}, u32[]{:S(2)}) collective-permute-start(bf16[64,1024]{1,0:T(8,128)(2,1)S(1)} %fusion.16), channel_id=1, source_target_pairs={{0,32},{1,33},{2,34},{3,35},{4,36},{5,37},{6,38},{7,39},{8,40},{9,... | collective-permute-start | bytes 393224 | tf_op jit(solution)/shard_map/ppermute | solution.py:24
  169.5 14.8 %copy-start.7 = (bf16[64,1024]{1,0:T(8,128)(2,1)S(1)}, bf16[64,1024]{1,0:T(8,128)(2,1)}, u32[]{:S(2)}) copy-start(bf16[64,1024]{1,0:T(8,128)(2,1)} %copy-done.6) | copy-start | bytes 393220
  169.5 7.0 %collective-permute-start.22 = (bf16[64,1024]{1,0:T(8,128)(2,1)S(1)}, bf16[64,1024]{1,0:T(8,128)(2,1)S(1)}, u32[]{:S(2)}, u32[]{:S(2)}) collective-permute-start(bf16[64,1024]{1,0:T(8,128)(2,1)S(1)} %fusion.17), channel_id=1, source_target_pairs={{0,32},{1,33},{2,34},{3,35},{4,36},{5,37},{6,38},{7,39},{8,40},{9,... | collective-permute-start | bytes 393224 | tf_op jit(solution)/shard_map/ppermute | solution.py:24
  177.2 6.3 %collective-permute-start.23 = (bf16[64,1024]{1,0:T(8,128)(2,1)S(1)}, bf16[64,1024]{1,0:T(8,128)(2,1)S(1)}, u32[]{:S(2)}, u32[]{:S(2)}) collective-permute-start(bf16[64,1024]{1,0:T(8,128)(2,1)S(1)} %fusion.18), channel_id=1, source_target_pairs={{0,32},{1,33},{2,34},{3,35},{4,36},{5,37},{6,38},{7,39},{8,40},{9,... | collective-permute-start | bytes 393224 | tf_op jit(solution)/shard_map/ppermute | solution.py:24
  184.3 6.3 %collective-permute-start.24 = (bf16[64,1024]{1,0:T(8,128)(2,1)S(1)}, bf16[64,1024]{1,0:T(8,128)(2,1)S(1)}, u32[]{:S(2)}, u32[]{:S(2)}) collective-permute-start(bf16[64,1024]{1,0:T(8,128)(2,1)S(1)} %fusion.19), channel_id=1, source_target_pairs={{0,32},{1,33},{2,34},{3,35},{4,36},{5,37},{6,38},{7,39},{8,40},{9,... | collective-permute-start | bytes 393224 | tf_op jit(solution)/shard_map/ppermute | solution.py:24
  184.4 10.9 %collective-permute-start.27 = (bf16[64,1024]{1,0:T(8,128)(2,1)S(1)}, bf16[64,1024]{1,0:T(8,128)(2,1)S(1)}, u32[]{:S(2)}, u32[]{:S(2)}) collective-permute-start(bf16[64,1024]{1,0:T(8,128)(2,1)S(1)} %copy-done.7), channel_id=1, source_target_pairs={{0,8},{1,9},{2,10},{3,11},{4,12},{5,13},{6,14},{7,15},{8,0},{9,1},... | collective-permute-start | bytes 393224 | tf_op jit(solution)/shard_map/ppermute | solution.py:24
  192.2 6.0 %collective-permute-start.25 = (bf16[64,1024]{1,0:T(8,128)(2,1)S(1)}, bf16[64,1024]{1,0:T(8,128)(2,1)S(1)}, u32[]{:S(2)}, u32[]{:S(2)}) collective-permute-start(bf16[64,1024]{1,0:T(8,128)(2,1)S(1)} %fusion.21), channel_id=1, source_target_pairs={{0,8},{1,9},{2,10},{3,11},{4,12},{5,13},{6,14},{7,15},{8,0},{9,1},... | collective-permute-start | bytes 393224 | tf_op jit(solution)/shard_map/ppermute | solution.py:24
  195.3 8.0 %collective-permute-start.28 = (bf16[128,1024]{1,0:T(8,128)(2,1)S(1)}, bf16[128,1024]{1,0:T(8,128)(2,1)S(1)}, u32[]{:S(2)}, u32[]{:S(2)}) collective-permute-start(bf16[128,1024]{1,0:T(8,128)(2,1)S(1)} %maximum_select_fusion.5), channel_id=1, source_target_pairs={{0,4},{1,5},{2,6},{3,7},{4,0},{5,1},{6,2},{7,3},{8,12},{9,13},{10,... | collective-permute-start | bytes 786440 | tf_op jit(solution)/shard_map/ppermute | solution.py:24
  198.2 8.1 %collective-permute-start.26 = (bf16[128,1024]{1,0:T(8,128)(2,1)S(1)}, bf16[128,1024]{1,0:T(8,128)(2,1)}, u32[]{:S(2)}, u32[]{:S(2)}) collective-permute-start(bf16[128,1024]{1,0:T(8,128)(2,1)S(1)} %maximum_select_fusion.4), channel_id=1, source_target_pairs={{0,4},{1,5},{2,6},{3,7},{4,0},{5,1},{6,2},{7,3},{8,12},{9,13},{10,... | collective-permute-start | bytes 786440 | tf_op jit(solution)/shard_map/ppermute | solution.py:24
  199.6 9.5 %collective-permute-start.29 = (bf16[128,1024]{1,0:T(8,128)(2,1)S(1)}, bf16[128,1024]{1,0:T(8,128)(2,1)S(1)}, u32[]{:S(2)}, u32[]{:S(2)}) collective-permute-start(bf16[128,1024]{1,0:T(8,128)(2,1)S(1)} %get-tuple-element.28.mine), channel_id=1, source_target_pairs={{0,4},{1,5},{2,6},{3,7},{4,0},{5,1},{6,2},{7,3},{8,12},{9,13},{10,... | collective-permute-start | bytes 786440 | tf_op jit(solution)/shard_map/ppermute | solution.py:24
  206.3 2.8 %copy-start.13 = (bf16[1024,1024]{1,0:T(8,128)(2,1)S(1)}, bf16[1024,1024]{1,0:T(8,128)(2,1)}, u32[]{:S(2)}) copy-start(bf16[1024,1024]{1,0:T(8,128)(2,1)} %copy-done.12) | copy-start | bytes 6291460
